TPU v7x, 32 devices: a whole 2x2x4 slice. The times are simulated.
32 devices in a mesh: frame: 8 (over z, x), head: 4 (over y, core).
Axes of the slice: x: 2, y: 2, z: 4, core: 2. Of those that a mesh axis runs over, the one named last changes fastest.
Arguments:
- queries: bfloat16 [16, 8, 32, 896], P('frame', None, None, 'head'), may hold values from -6 to 6
- key_vectors: bfloat16 [16, 8, 32, 896], P('frame', None, None, 'head'), may hold values from -6 to 6
- value_vectors: bfloat16 [16, 8, 32, 896], P('frame', None, None, 'head'), may hold values from -8 to 8
- frame_index: int32 [16], P('frame'), may hold values from 0 to 31, as said below
- height_index: int32 [8], replicated, may hold values from 0 to 15, as said below
- width_index: int32 [32], replicated, may hold values from 0 to 63, as said below
- frame_block: int32 [16], P('frame'), may hold values from 0 to 4, never falling along the last dimension, each value on 1 to 6 neighbouring positions
- conv_weight: bfloat16 [3, 896, 2240], P(None, 'head'), may hold values from -0.125 to 0.125
- conv_bias: float32 [2240], replicated, may hold values from -0.8 to 0.8
Outputs:
- mixed_frames: bfloat16 [8, 16, 32, 2240], P('head', 'frame')
Inputs may be any that keep to these rules, and one draw needn't show every extreme that they name: `frame_index`: strictly increasing over the frames, first entry 0, last entry 31. `height_index`: strictly increasing over the rows, first entry 0, last entry 15. `width_index`: strictly increasing over the columns, first entry 0, last entry 63.
All inputs are finite; a program needn't handle non-finite values.
Results may differ from a plain program's by a relative error of at most 0.0043.
The roundings to bfloat16 on the way count: a program that leaves them out, or rounds other values in their place, can miss the bound.
Values may be sent and summed in bfloat16 or wider, within the bound.
A program may use at most 128 MiB of HBM per device.

v0:
```python
import functools

import jax
import jax.numpy as jnp
import numpy as np
from jax import lax
from jax.experimental import pallas as pl
from jax.experimental.pallas import tpu as pltpu
from jax.sharding import PartitionSpec as P

HD = 112
PAD = 128
EPSILON = 1e-06
BLOCK_MOST = 6
COLUMNS = 512
F32 = jnp.float32
BF16 = jnp.bfloat16


def sections():
    side = HD * 5 // 14 // 2 * 2
    first = HD - 2 * side
    return ((0, first), (first, side), (first + side, side))


def tables(heads):
    C, lanes = heads * HD, heads * PAD
    lane = lax.broadcasted_iota(jnp.int32, (1, lanes), 1)
    head, d = lane // PAD, lane % PAD
    inside = d < HD
    source = jnp.where(inside, head * HD + d, -1)
    partner, sign = jnp.full_like(lane, -1), jnp.zeros((1, lanes), F32)
    freqs, masks = [], []
    for start, n in sections():
        half = n // 2
        low = (d >= start) & (d < start + half)
        high = (d >= start + half) & (d < start + n)
        partner = jnp.where(low, source + half, jnp.where(high, source - half, partner))
        sign = jnp.where(low, -1.0, jnp.where(high, 1.0, sign))
        j = jnp.where(low, d - start, d - start - half).astype(F32)
        either = low | high
        freqs.append(jnp.where(either, jnp.exp(j * float(-2.0 * np.log(10000.0) / n)), 0.0))
        masks.append(jnp.where(either, 1.0, 0.0))
    row = lax.broadcasted_iota(jnp.int32, (C, lanes), 0)
    spread = jnp.where(row == source, 1.0, 0.0).astype(BF16)
    swap = jnp.where(row == partner, sign, 0.0).astype(BF16)
    column = lax.broadcasted_iota(jnp.int32, (1, C), 1)
    target = column // HD * PAD + column % HD
    row = lax.broadcasted_iota(jnp.int32, (lanes, C), 0)
    gather = jnp.where(row == target, 1.0, 0.0).astype(BF16)
    return spread, swap, gather, freqs, masks


def positions(ref, count, rows, lanes):
    row = lax.broadcasted_iota(jnp.int32, (rows, lanes), 0)
    result = jnp.zeros((rows, lanes), F32)
    for i in range(count):
        result = jnp.where(row == i, ref[i].astype(F32), result)
    return result


def mm(a, b):
    return jnp.dot(a, b, preferred_element_type=F32)


def mm_t(a, b):
    return lax.dot_general(a, b, (((0,), (0,)), ((), ())), preferred_element_type=F32)


def mm_n(a, b):
    return lax.dot_general(a, b, (((1,), (1,)), ((), ())), preferred_element_type=F32)


def split(a):
    high = a.astype(BF16)
    return high, (a - high.astype(F32)).astype(BF16)


def kernel(
    cfg, q_any, k_any, v_any, fi_any, hi_any, wi_any, fb_any, w_ref, bias_any, out_ref,
    q_ref, k_ref, v_ref, fi_ref, hi_ref, wi_ref, fb_ref, bias_ref, in_sem, w_buf, qh, time_own, time_prev, msg_t, msg_l, msg_n, msg_r, msg_j, recv_t, recv_l, recv_n, recv_r, recv_j, base, state, att, att_x, *rest,
):
    F, Y, heads, HG, W, chunks = cfg
    n_chunk = len(chunks)
    part_send, part_recv, part_own = rest[:n_chunk], rest[n_chunk : 2 * n_chunk], rest[2 * n_chunk : 3 * n_chunk]
    (w_sem, w_send, w_recv, halo_send, halo_recv, t_send, t_recv, l_send, l_recv, p_send, p_recv,
          x_send, x_recv, c_send, c_recv) = rest[3 * n_chunk :]
    FC = 2
    H = 2 * Y
    TF = HG * W
    RD = HG // H
    TD = RD * W
    O = F // 2
    reach = -(-(BLOCK_MOST - 1) // FC)
    down = (reach + 1) // 2
    f = lax.axis_index("frame")
    h = lax.axis_index("head")
    y, c = h // 2, h % 2
    mate = 2 * y + (1 - c)
    inner, outer = f % 2, f // 2
    partner = f + 1 - 2 * inner

    loads = [
        pltpu.make_async_copy(src, dst, in_sem.at[i])
        for i, (src, dst) in enumerate(
            [(fi_any, fi_ref), (hi_any, hi_ref), (wi_any, wi_ref), (fb_any, fb_ref), (k_any, k_ref), (v_any, v_ref),
             (q_any, q_ref), (bias_any, bias_ref)]
        )
    ]
    for load in loads:
        load.start()

    barrier = pltpu.get_barrier_semaphore()
    for k in range(1, F):
        pl.semaphore_signal(barrier, inc=1, device_id=(lax.rem(f + k, F), h), device_id_type=pl.DeviceIdType.MESH)
    pl.semaphore_signal(barrier, inc=1, device_id=(f, mate), device_id_type=pl.DeviceIdType.MESH)
    for j in range(1, Y):
        pl.semaphore_signal(
            barrier, inc=1, device_id=(f, 2 * lax.rem(y + j, Y) + c), device_id_type=pl.DeviceIdType.MESH
        )

    def remote(src, dst, send, recv, frame, head):
        return pltpu.make_async_remote_copy(
            src_ref=src, dst_ref=dst, send_sem=send, recv_sem=recv,
            device_id=(frame, head), device_id_type=pl.DeviceIdType.MESH,
        )

    w_local = pltpu.make_async_copy(w_ref, w_buf.at[0], w_sem)
    w_local.start()

    lanes = heads * PAD
    spread, swap, gather, freqs, masks = tables(heads)
    for load in loads[:4]:
        load.wait()
    t_ang = positions(fi_ref, FC, 8, lanes) * freqs[0]
    time_own[0:8, :] = jnp.cos(t_ang) * masks[0]
    time_own[8:16, :] = jnp.sin(t_ang)
    h_ang = positions(hi_ref, HG, HG, lanes) * freqs[1]
    w_ang = positions(wi_ref, W, W, lanes) * freqs[2]
    cos_hw = (
        (jnp.cos(h_ang) * masks[1]).reshape(HG, 1, lanes) + (jnp.cos(w_ang) * masks[2]).reshape(1, W, lanes)
    ).reshape(TF, lanes)
    sin_hw = (jnp.sin(h_ang).reshape(HG, 1, lanes) + jnp.sin(w_ang).reshape(1, W, lanes)).reshape(TF, lanes)

    pl.semaphore_wait(barrier, (F - 1) + 1 + (Y - 1))

    w_far = remote(w_ref, w_buf.at[1], w_send, w_recv, f, mate)
    w_far.start()
    nxt = lax.rem(f + 1, F)
    q_copy = remote(q_any, qh, halo_send.at[0], halo_recv.at[0], nxt, h)
    t_copy = remote(time_own, time_prev, halo_send.at[1], halo_recv.at[1], nxt, h)

    @pl.when(f < F - 1)
    def _():
        q_copy.start()
        t_copy.start()

    @pl.when(f == 0)
    def _():
        qh[...] = jnp.zeros_like(qh)
        time_prev[...] = jnp.zeros_like(time_prev)
        recv_n[...] = jnp.zeros_like(recv_n)


    def rotated(rows, cos_t, sin_t):
        positive = jnp.maximum(rows, jnp.zeros_like(rows))
        plain = mm(positive, spread)
        turned = mm(positive, swap)
        return plain.astype(BF16), plain * (cos_hw + cos_t) + turned * (sin_hw + sin_t)

    ones = jnp.where(lax.broadcasted_iota(jnp.int32, (PAD, TF), 0) >= HD, 1.0, 0.0).astype(BF16)
    for load in loads[4:6]:
        load.wait()
    frames = []
    for t in range(FC):
        rows = slice(t * TF, (t + 1) * TF)
        k_pos, k_rot = rotated(k_ref[rows, :], time_own[t : t + 1, :], time_own[8 + t : 9 + t, :])
        k_hi, k_lo = split(k_rot)
        value = mm(v_ref[rows, :], spread).astype(BF16)
        per_head = []
        totals = mm(ones, k_pos)
        for g in range(heads):
            cut = slice(g * PAD, (g + 1) * PAD)
            both = mm_t(value[:, cut], jnp.concatenate([k_hi[:, cut], k_lo[:, cut]], axis=1))
            per_head.append(both[:, :PAD] + both[:, PAD:] + totals[:, cut])
        frames.append(jnp.concatenate(per_head, axis=0))
    id0 = fb_ref[0].astype(F32)
    id1 = fb_ref[1].astype(F32)
    same = jnp.where(id0 == id1, 1.0, 0.0)
    own_t = frames[0] + frames[1]
    own_l = frames[0] + same * frames[1]
    row = lax.broadcasted_iota(jnp.int32, own_t.shape, 0)

    def tagged(value, first, second):
        return jnp.where(row == HD + 1, first, jnp.where(row == HD + 2, second, value)).astype(BF16)

    msg_t[...] = own_t.astype(BF16)
    msg_l[...] = tagged(own_l, id0, id1)
    msg_n[...] = tagged((same - 1.0) * frames[1], id0, id1)

    t_copies, l_copies, l_sends, l_gets = {}, {}, {}, {}
    for k in range(1, O):
        t_copies[k] = remote(
            msg_t, recv_t.at[k - 1], t_send.at[k - 1], t_recv.at[k - 1], lax.rem(f + 2 * k, F), h
        )
    for k in range(1, down + 1):
        l_copies[k] = remote(
            msg_l, recv_l.at[k - 1], l_send.at[k - 1], l_recv.at[k - 1], lax.rem(f - 2 * k + 2 * F, F), h
        )
        wanted = 2 * k <= reach + 1 - inner
        l_sends[k] = wanted & (outer >= k)
        l_gets[k] = wanted & (outer + k < O)
    n_copy = remote(msg_n, recv_n, p_send.at[0], p_recv.at[0], nxt, h)
    r_copy = remote(msg_r, recv_r, p_send.at[1], p_recv.at[1], partner, h)
    j_copy = remote(msg_j, recv_j, p_send.at[2], p_recv.at[2], partner, h)
    for k in range(O - 1, 0, -1):

        @pl.when(outer + k < O)
        def _(k=k):
            t_copies[k].start()

    for k in range(down, 0, -1):

        @pl.when(l_sends[k])
        def _(k=k):
            l_copies[k].start()

    @pl.when(f < F - 1)
    def _():
        n_copy.start()

    loads[6].wait()
    q_parts = [None, None]
    for t in range(FC):
        rows = slice(t * TF, (t + 1) * TF)
        q_parts.append(rotated(q_ref[rows, :], time_own[t : t + 1, :], time_own[8 + t : 9 + t, :]))

    @pl.when(inner == 0)
    def _():
        base[...] = own_t

    @pl.when(inner == 1)
    def _():
        base[...] = jnp.zeros_like(own_t)

    for k in range(1, O):

        @pl.when(outer >= k)
        def _(k=k):
            t_copies[k].wait_recv()
            base[...] += recv_t[k - 1].astype(F32)

    msg_r[...] = base[...].astype(BF16)
    r_copy.start()

    for k in range(1, down + 1):

        @pl.when(l_gets[k])
        def _(k=k):
            l_copies[k].wait_recv()

        @pl.when(jnp.logical_not(l_gets[k]))
        def _(k=k):
            recv_l[k - 1] = tagged(jnp.zeros_like(own_t), -1.0, -1.0)

    def joined(ident, total, pieces):
        for piece in pieces:
            total = total + jnp.where(piece[HD + 1 : HD + 2] == ident, 1.0, 0.0) * piece
        return tagged(total, ident, ident)

    leads = [recv_l[k].astype(F32) for k in range(down)]

    @pl.when(inner == 0)
    def _():
        msg_j[...] = joined(leads[0][HD + 1 : HD + 2], leads[0], leads[1:])

    @pl.when(inner == 1)
    def _():
        msg_j[...] = joined(id0, own_l, leads[:1])

    j_copy.start()

    @pl.when(f > 0)
    def _():
        q_copy.wait_recv()
        t_copy.wait_recv()

    for t in range(FC):
        rows = slice(t * TF, (t + 1) * TF)
        q_parts[t] = rotated(qh[rows, :], time_prev[t : t + 1, :], time_prev[8 + t : 9 + t, :])

    @pl.when(f > 0)
    def _():
        n_copy.wait_recv()

    r_copy.wait_recv()
    j_copy.wait_recv()
    before = base[...] + recv_r[...].astype(F32) - jnp.where(inner == 0, 1.0, 0.0) * own_t
    less = recv_n[...].astype(F32)
    tails = [recv_j[...].astype(F32)] + leads
    ids = [less[HD + 1 : HD + 2], less[HD + 2 : HD + 3], id0, id1]
    starts = [before + less, before, before + own_l, before + own_t]
    for i in range(2 + FC):
        total = starts[i]
        if i < 2:
            total = total + jnp.where(ids[i] == id0, 1.0, 0.0) * own_l
        for tail in tails:
            total = total + jnp.where(tail[HD + 1 : HD + 2] == ids[i], 1.0, 0.0) * tail
        state[i] = total

    for t in range(2 + FC):
        q_pos, q_rot = q_parts[t]
        q_hi, q_lo = split(q_rot)
        full = state[t]
        merged = []
        for g in range(heads):
            cut = slice(g * PAD, (g + 1) * PAD)
            block = full[cut, :]
            s_hi, s_lo = split(block)
            total_hi, total_lo = split(jnp.broadcast_to(block[HD : HD + 1, :], (PAD, PAD)))
            both = mm_n(q_hi[:, cut], jnp.concatenate([s_hi, s_lo], axis=0))
            numerator = both[:, :PAD] + both[:, PAD:] + mm_n(q_lo[:, cut], s_hi)
            both = mm_n(q_pos[:, cut], jnp.concatenate([total_hi, total_lo], axis=0))
            denominator = both[:, :PAD] + both[:, PAD:] + EPSILON
            merged.append((numerator / denominator).astype(BF16))
        tight = mm(jnp.concatenate(merged, axis=1), gather).astype(BF16)
        for g in range(H):
            att[g, t] = tight[g * TD : (g + 1) * TD]

    x_copies = []
    for j in range(Y):
        x_copies.append(remote(att.at[2 * j + 1 - c], att_x.at[j], x_send.at[j], x_recv.at[j], f, mate))
        x_copies[-1].start()
    w_local.wait()
    w_far.wait_recv()
    for copy in x_copies:
        copy.wait_recv()

    starts = np.cumsum([0] + list(chunks))
    owners = [lax.rem(y + j, Y) for j in range(1, Y)] + [y]
    M = FC * TD
    taps = []
    for tap in range(3):
        for side in range(2):
            rows = [(att.at[2 * j + c] if side == 0 else att_x.at[j])[2 - tap : 2 - tap + FC] for j in owners]
            taps.append((tap, side, jnp.concatenate([r.reshape(M, heads * HD) for r in rows], axis=0)))

    c_copies = {}
    for n in range(n_chunk):
        cols = slice(int(starts[n]), int(starts[n + 1]))
        total = None
        for tap, side, rows in taps:
            term = mm(rows, w_buf[side, tap, :, cols])
            total = term if total is None else total + term
        for j in range(1, Y):
            part_send[n][j - 1] = total[(j - 1) * M : j * M].astype(BF16)
            slot = (j - 1) * n_chunk + n
            c_copies[j, n] = remote(
                part_send[n].at[j - 1], part_recv[n].at[j - 1], c_send.at[slot], c_recv.at[slot], f,
                2 * owners[j - 1] + c,
            )
            c_copies[j, n].start()
        part_own[n][...] = total[(Y - 1) * M :]
    loads[7].wait()
    bias = bias_ref[...].reshape(1, -1)
    for n in range(n_chunk):
        cols = slice(int(starts[n]), int(starts[n + 1]))
        total = part_own[n][...]
        for j in range(1, Y):
            c_copies[j, n].wait_recv()
            total = total + part_recv[n][j - 1].astype(F32)
        total = total + bias[:, cols]
        result = (total / (1.0 + jnp.exp(-total))).astype(BF16)
        for t in range(FC):
            for r in range(RD):
                start = t * TD + r * W
                out_ref[r, t, :, cols] = result[start : start + W]

    w_far.wait_send()
    for copy in x_copies + list(c_copies.values()):
        copy.wait_send()

    @pl.when(f < F - 1)
    def _():
        q_copy.wait_send()
        t_copy.wait_send()
        n_copy.wait_send()

    r_copy.wait_send()
    j_copy.wait_send()
    for k in range(1, O):

        @pl.when(outer + k < O)
        def _(k=k):
            t_copies[k].wait_send()

    for k in range(1, down + 1):

        @pl.when(l_sends[k])
        def _(k=k):
            l_copies[k].wait_send()


def per_device(F, H, queries, key_vectors, value_vectors, frame_index, height_index, width_index, frame_block,
               conv_weight, conv_bias):
    FC, HG, W, C = queries.shape
    heads = C // HD
    assert FC == 2 and H % 2 == 0 and F % 2 == 0
    Y = H // 2
    T, TF, RD = FC * HG * W, HG * W, HG // H
    TD = RD * W
    O = conv_weight.shape[-1]
    chunks = [COLUMNS] * (O // COLUMNS) + ([O % COLUMNS] if O % COLUMNS else [])
    outer = max(F // 2 - 1, 1)
    down = (-(-(BLOCK_MOST - 1) // FC) + 1) // 2
    lanes = heads * PAD
    vmem = pl.BlockSpec(memory_space=pltpu.VMEM)
    dma = pltpu.SemaphoreType.DMA
    return pl.pallas_call(
        functools.partial(kernel, (F, Y, heads, HG, W, tuple(chunks))),
        out_shape=jax.ShapeDtypeStruct((RD, FC, W, O), BF16),
        in_specs=[pl.BlockSpec(memory_space=pl.ANY)] * 9,
        out_specs=vmem,
        scratch_shapes=[
            pltpu.VMEM((T, C), BF16),
            pltpu.VMEM((T, C), BF16),
            pltpu.VMEM((T, C), BF16),
            pltpu.SMEM((FC,), jnp.int32),
            pltpu.SMEM((HG,), jnp.int32),
            pltpu.SMEM((W,), jnp.int32),
            pltpu.SMEM((FC,), jnp.int32),
            pltpu.VMEM((O,), F32),
            dma((8,)),
            pltpu.VMEM((2,) + conv_weight.shape, BF16),
            pltpu.VMEM((T, C), BF16),
            pltpu.VMEM((16, lanes), F32),
            pltpu.VMEM((16, lanes), F32),
            *[pltpu.VMEM((lanes, PAD), BF16)] * 5,
            pltpu.VMEM((outer, lanes, PAD), BF16),
            pltpu.VMEM((down, lanes, PAD), BF16),
            *[pltpu.VMEM((lanes, PAD), BF16)] * 3,
            pltpu.VMEM((lanes, PAD), F32),
            pltpu.VMEM((4, lanes, PAD), F32),
            pltpu.VMEM((H, 2 + FC, TD, C), BF16),
            pltpu.VMEM((Y, 2 + FC, TD, C), BF16),
        ]
        + [pltpu.VMEM((max(Y - 1, 1), FC * TD, n), BF16) for n in chunks]
        + [pltpu.VMEM((max(Y - 1, 1), FC * TD, n), BF16) for n in chunks]
        + [pltpu.VMEM((FC * TD, n), F32) for n in chunks]
        + [
            dma, dma, dma, dma((2,)), dma((2,)),
            dma((outer,)), dma((outer,)), dma((down,)), dma((down,)), dma((3,)), dma((3,)),
            dma((Y,)), dma((Y,)),
            dma((max(Y - 1, 1) * len(chunks),)), dma((max(Y - 1, 1) * len(chunks),)),
        ],
        compiler_params=pltpu.CompilerParams(
            collective_id=0, has_side_effects=True, vmem_limit_bytes=60 * 1024 * 1024
        ),
        name="attend_conv",
    )(
        queries.reshape(T, C),
        key_vectors.reshape(T, C),
        value_vectors.reshape(T, C),
        frame_index,
        height_index,
        width_index,
        frame_block,
        conv_weight,
        conv_bias,
    )


def solution(mesh):
    placed = (
        P("frame", None, None, "head"),
        P("frame", None, None, "head"),
        P("frame", None, None, "head"),
        P("frame"),
        P(),
        P(),
        P("frame"),
        P(None, "head", None),
        P(),
    )
    return jax.shard_map(
        functools.partial(per_device, mesh.shape["frame"], mesh.shape["head"]),
        mesh=mesh,
        in_specs=placed,
        out_specs=P("head", "frame", None, None),
        check_vma=False,
    )
```

profile of v0, /device:TPU:17, one launch (start us, length us, event | category | flops | bytes accessed | tf_op | source)
XLA Modules:
  0.0 41.3 jit_solution(4724299395836740216)
XLA Ops:
  0.0 39.4 %attend_conv.1 = bf16[2,2,32,2240]{3,2,1,0:T(8,128)(2,1)} custom-call(bf16[512,224]{1,0:T(8,128)(2,1)} %bitcast.3, bf16[512,224]{1,0:T(8,128)(2,1)} %bitcast.4, bf16[512,224]{1,0:T(8,128)(2,1)} %bitcast.5, s32[2]{0:T(128)} %fi_any.1, s32[8]{0:T(128)} %hi_any.1, s32[32]{0:T(128)} %wi_any.1, s32[2]{0:T(128)} %fb_any.1, bf16[3,224,2240]{2,1,0:T(8,128)(2,1)} %w_ref.1, ...), custom_call_target="tpu_custom_call" | custom-call | tf_op jit(solution)/shard_map/attend_conv/pallas_call | solution.py:419
  39.4 1.9 %copy.11 = bf16[2,2,32,2240]{3,2,1,0:T(8,128)(2,1)} copy(bf16[2,2,32,2240]{3,2,1,0:T(8,128)(2,1)} %attend_conv.1) | data formatting | bytes 1146880
where the time goes:
time: 41.5 us; the launch traced here: 41.3 us
  Pallas kernels  39.4 us (95%)
  local copies, waits for them, and re-layouts  1.92 us (5%)
    pallas_call x1, Pallas kernels, per_device(): pl.pallas_call(functools.partial(kernel, (F, Y, heads, HG, W, tuple(chunk...  39.4 us
    unnamed x1, local copies, waits for them, and re-layouts  1.92 us

commit v1 on v0

--- a/solution.py
+++ b/solution.py
@@ -145,7 +145,6 @@
     pl.semaphore_wait(barrier, (F - 1) + 1 + (Y - 1))
 
     w_far = remote(w_ref, w_buf.at[1], w_send, w_recv, f, mate)
-    w_far.start()
     nxt = lax.rem(f + 1, F)
     q_copy = remote(q_any, qh, halo_send.at[0], halo_recv.at[0], nxt, h)
     t_copy = remote(time_own, time_prev, halo_send.at[1], halo_recv.at[1], nxt, h)
@@ -213,6 +212,10 @@
     n_copy = remote(msg_n, recv_n, p_send.at[0], p_recv.at[0], nxt, h)
     r_copy = remote(msg_r, recv_r, p_send.at[1], p_recv.at[1], partner, h)
     j_copy = remote(msg_j, recv_j, p_send.at[2], p_recv.at[2], partner, h)
+    @pl.when(f < F - 1)
+    def _():
+        n_copy.start()
+
     for k in range(O - 1, 0, -1):
 
         @pl.when(outer + k < O)
@@ -225,9 +228,7 @@
         def _(k=k):
             l_copies[k].start()
 
-    @pl.when(f < F - 1)
-    def _():
-        n_copy.start()
+    w_far.start()
 
     loads[6].wait()
     q_parts = [None, None]

time: 41.5 us -> 42.1 us (1.014)
  Pallas kernels: 39.4 us -> 40.1 us
    pallas_call x1, Pallas kernels: 39.4 us -> 40.1 us  [per_device(): pl.pallas_call(functools.partial(kernel, (F, Y, heads, HG, W, tuple(chunk...]
where the time goes in v1:
time: 42.1 us; the launch traced here: 42 us
  Pallas kernels  40.1 us (95%)
  local copies, waits for them, and re-layouts  1.92 us (5%)
    pallas_call x1, Pallas kernels, per_device(): pl.pallas_call(functools.partial(kernel, (F, Y, heads, HG, W, tuple(chunk...  40.1 us
    unnamed x1, local copies, waits for them, and re-layouts  1.92 us

profile of v1, /device:TPU:17, one launch (start us, length us, event | category | flops | bytes accessed | tf_op | source)
XLA Modules:
  0.0 42.0 jit_solution(3258926047175989055)
XLA Ops:
  0.0 40.1 %attend_conv.1 = bf16[2,2,32,2240]{3,2,1,0:T(8,128)(2,1)} custom-call(bf16[512,224]{1,0:T(8,128)(2,1)} %bitcast.3, bf16[512,224]{1,0:T(8,128)(2,1)} %bitcast.4, bf16[512,224]{1,0:T(8,128)(2,1)} %bitcast.5, s32[2]{0:T(128)} %fi_any.1, s32[8]{0:T(128)} %hi_any.1, s32[32]{0:T(128)} %wi_any.1, s32[2]{0:T(128)} %fb_any.1, bf16[3,224,2240]{2,1,0:T(8,128)(2,1)} %w_ref.1, ...), custom_call_target="tpu_custom_call" | custom-call | tf_op jit(solution)/shard_map/attend_conv/pallas_call | solution.py:420
  40.1 1.9 %copy.11 = bf16[2,2,32,2240]{3,2,1,0:T(8,128)(2,1)} copy(bf16[2,2,32,2240]{3,2,1,0:T(8,128)(2,1)} %attend_conv.1) | data formatting | bytes 1146880

commit v2 on v1

--- a/solution.py
+++ b/solution.py
@@ -128,6 +128,17 @@
     w_local = pltpu.make_async_copy(w_ref, w_buf.at[0], w_sem)
     w_local.start()
 
+    pl.semaphore_wait(barrier, (F - 1) + 1 + (Y - 1))
+
+    w_far = remote(w_ref, w_buf.at[1], w_send, w_recv, f, mate)
+    nxt = lax.rem(f + 1, F)
+    q_copy = remote(q_any, qh, halo_send.at[0], halo_recv.at[0], nxt, h)
+    t_copy = remote(time_own, time_prev, halo_send.at[1], halo_recv.at[1], nxt, h)
+
+    @pl.when(f < F - 1)
+    def _():
+        q_copy.start()
+
     lanes = heads * PAD
     spread, swap, gather, freqs, masks = tables(heads)
     for load in loads[:4]:
@@ -142,16 +153,8 @@
     ).reshape(TF, lanes)
     sin_hw = (jnp.sin(h_ang).reshape(HG, 1, lanes) + jnp.sin(w_ang).reshape(1, W, lanes)).reshape(TF, lanes)
 
-    pl.semaphore_wait(barrier, (F - 1) + 1 + (Y - 1))
-
-    w_far = remote(w_ref, w_buf.at[1], w_send, w_recv, f, mate)
-    nxt = lax.rem(f + 1, F)
-    q_copy = remote(q_any, qh, halo_send.at[0], halo_recv.at[0], nxt, h)
-    t_copy = remote(time_own, time_prev, halo_send.at[1], halo_recv.at[1], nxt, h)
-
     @pl.when(f < F - 1)
     def _():
-        q_copy.start()
         t_copy.start()
 
     @pl.when(f == 0)
@@ -193,15 +196,28 @@
     def tagged(value, first, second):
         return jnp.where(row == HD + 1, first, jnp.where(row == HD + 2, second, value)).astype(BF16)
 
-    msg_t[...] = own_t.astype(BF16)
+    msg_t[0] = own_t.astype(BF16)
     msg_l[...] = tagged(own_l, id0, id1)
     msg_n[...] = tagged((same - 1.0) * frames[1], id0, id1)
 
     t_copies, l_copies, l_sends, l_gets = {}, {}, {}, {}
-    for k in range(1, O):
-        t_copies[k] = remote(
-            msg_t, recv_t.at[k - 1], t_send.at[k - 1], t_recv.at[k - 1], lax.rem(f + 2 * k, F), h
-        )
+    steps = (O - 1).bit_length()
+    for i in range(steps):
+        for k in range(1, 2**i + 1):
+            t_copies[i, k] = remote(
+                msg_t.at[i], recv_t.at[i], t_send.at[2**i + k - 2], t_recv.at[i], lax.rem(f + 2 * k, F), h
+            )
+
+    def t_sends(i, k):
+        return (outer % 2 ** (i + 1) == 2**i - 1) & (outer + k < O)
+
+    def t_start(i):
+        for k in range(2**i, 0, -1):
+
+            @pl.when(t_sends(i, k))
+            def _(k=k):
+                t_copies[i, k].start()
+
     for k in range(1, down + 1):
         l_copies[k] = remote(
             msg_l, recv_l.at[k - 1], l_send.at[k - 1], l_recv.at[k - 1], lax.rem(f - 2 * k + 2 * F, F), h
@@ -216,11 +232,7 @@
     def _():
         n_copy.start()
 
-    for k in range(O - 1, 0, -1):
-
-        @pl.when(outer + k < O)
-        def _(k=k):
-            t_copies[k].start()
+    t_start(0)
 
     for k in range(down, 0, -1):
 
@@ -236,22 +248,20 @@
         rows = slice(t * TF, (t + 1) * TF)
         q_parts.append(rotated(q_ref[rows, :], time_own[t : t + 1, :], time_own[8 + t : 9 + t, :]))
 
-    @pl.when(inner == 0)
-    def _():
-        base[...] = own_t
-
-    @pl.when(inner == 1)
-    def _():
-        base[...] = jnp.zeros_like(own_t)
-
-    for k in range(1, O):
-
-        @pl.when(outer >= k)
-        def _(k=k):
-            t_copies[k].wait_recv()
-            base[...] += recv_t[k - 1].astype(F32)
-
-    msg_r[...] = base[...].astype(BF16)
+    base[...] = jnp.zeros_like(own_t)
+    for i in range(steps):
+
+        @pl.when(outer // 2**i % 2 == 1)
+        def _(i=i):
+            t_copies[i, 1].wait_recv()
+            base[...] += recv_t[i].astype(F32)
+
+        if i + 1 < steps:
+            msg_t[i + 1] = (base[...] + own_t).astype(BF16)
+            t_start(i + 1)
+
+    earlier = base[...]
+    msg_r[...] = (earlier + jnp.where(inner == 0, 1.0, 0.0) * own_t).astype(BF16)
     r_copy.start()
 
     for k in range(1, down + 1):
@@ -296,7 +306,7 @@
 
     r_copy.wait_recv()
     j_copy.wait_recv()
-    before = base[...] + recv_r[...].astype(F32) - jnp.where(inner == 0, 1.0, 0.0) * own_t
+    before = earlier + recv_r[...].astype(F32)
     less = recv_n[...].astype(F32)
     tails = [recv_j[...].astype(F32)] + leads
     ids = [less[HD + 1 : HD + 2], less[HD + 2 : HD + 3], id0, id1]
@@ -389,11 +399,11 @@
 
     r_copy.wait_send()
     j_copy.wait_send()
-    for k in range(1, O):
-
-        @pl.when(outer + k < O)
-        def _(k=k):
-            t_copies[k].wait_send()
+    for i, k in t_copies:
+
+        @pl.when(t_sends(i, k))
+        def _(i=i, k=k):
+            t_copies[i, k].wait_send()
 
     for k in range(1, down + 1):
 
@@ -412,7 +422,7 @@
     TD = RD * W
     O = conv_weight.shape[-1]
     chunks = [COLUMNS] * (O // COLUMNS) + ([O % COLUMNS] if O % COLUMNS else [])
-    outer = max(F // 2 - 1, 1)
+    steps = max((F // 2 - 1).bit_length(), 1)
     down = (-(-(BLOCK_MOST - 1) // FC) + 1) // 2
     lanes = heads * PAD
     vmem = pl.BlockSpec(memory_space=pltpu.VMEM)
@@ -436,8 +446,9 @@
             pltpu.VMEM((T, C), BF16),
             pltpu.VMEM((16, lanes), F32),
             pltpu.VMEM((16, lanes), F32),
-            *[pltpu.VMEM((lanes, PAD), BF16)] * 5,
-            pltpu.VMEM((outer, lanes, PAD), BF16),
+            pltpu.VMEM((steps, lanes, PAD), BF16),
+            *[pltpu.VMEM((lanes, PAD), BF16)] * 4,
+            pltpu.VMEM((steps, lanes, PAD), BF16),
             pltpu.VMEM((down, lanes, PAD), BF16),
             *[pltpu.VMEM((lanes, PAD), BF16)] * 3,
             pltpu.VMEM((lanes, PAD), F32),
@@ -450,7 +461,7 @@
         + [pltpu.VMEM((FC * TD, n), F32) for n in chunks]
         + [
             dma, dma, dma, dma((2,)), dma((2,)),
-            dma((outer,)), dma((outer,)), dma((down,)), dma((down,)), dma((3,)), dma((3,)),
+            dma((2**steps,)), dma((steps,)), dma((down,)), dma((down,)), dma((3,)), dma((3,)),
             dma((Y,)), dma((Y,)),
             dma((max(Y - 1, 1) * len(chunks),)), dma((max(Y - 1, 1) * len(chunks),)),
         ],

time: 42.1 us -> 42.3 us (level)
  no operation moved by 1% of the time
where the time goes in v2:
time: 42.3 us; the launch traced here: 42.2 us
  Pallas kernels  40.3 us (95%)
  local copies, waits for them, and re-layouts  1.92 us (5%)
    pallas_call x1, Pallas kernels, per_device(): pl.pallas_call(functools.partial(kernel, (F, Y, heads, HG, W, tuple(chunk...  40.3 us
    unnamed x1, local copies, waits for them, and re-layouts  1.92 us

profile of v2, /device:TPU:17, one launch (start us, length us, event | category | flops | bytes accessed | tf_op | source)
XLA Modules:
  0.0 42.2 jit_solution(3034759773441735148)
XLA Ops:
  0.0 40.3 %attend_conv.1 = bf16[2,2,32,2240]{3,2,1,0:T(8,128)(2,1)} custom-call(bf16[512,224]{1,0:T(8,128)(2,1)} %bitcast.3, bf16[512,224]{1,0:T(8,128)(2,1)} %bitcast.4, bf16[512,224]{1,0:T(8,128)(2,1)} %bitcast.5, s32[2]{0:T(128)} %fi_any.1, s32[8]{0:T(128)} %hi_any.1, s32[32]{0:T(128)} %wi_any.1, s32[2]{0:T(128)} %fb_any.1, bf16[3,224,2240]{2,1,0:T(8,128)(2,1)} %w_ref.1, ...), custom_call_target="tpu_custom_call" | custom-call | tf_op jit(solution)/shard_map/attend_conv/pallas_call | solution.py:430
  40.3 1.9 %copy.11 = bf16[2,2,32,2240]{3,2,1,0:T(8,128)(2,1)} copy(bf16[2,2,32,2240]{3,2,1,0:T(8,128)(2,1)} %attend_conv.1) | data formatting | bytes 1146880

commit v3 on v2

--- a/solution.py
+++ b/solution.py
@@ -242,54 +242,54 @@
 
     w_far.start()
 
+    base[...] = jnp.zeros_like(own_t)
+    for i in range(steps):
+
+        @pl.when(outer // 2**i % 2 == 1)
+        def _(i=i):
+            t_copies[i, 1].wait_recv()
+            base[...] += recv_t[i].astype(F32)
+
+        if i + 1 < steps:
+            msg_t[i + 1] = (base[...] + own_t).astype(BF16)
+            t_start(i + 1)
+
+    earlier = base[...]
+    msg_r[...] = (earlier + jnp.where(inner == 0, 1.0, 0.0) * own_t).astype(BF16)
+    r_copy.start()
+
+    for k in range(1, down + 1):
+
+        @pl.when(l_gets[k])
+        def _(k=k):
+            l_copies[k].wait_recv()
+
+        @pl.when(jnp.logical_not(l_gets[k]))
+        def _(k=k):
+            recv_l[k - 1] = tagged(jnp.zeros_like(own_t), -1.0, -1.0)
+
+    def joined(ident, total, pieces):
+        for piece in pieces:
+            total = total + jnp.where(piece[HD + 1 : HD + 2] == ident, 1.0, 0.0) * piece
+        return tagged(total, ident, ident)
+
+    leads = [recv_l[k].astype(F32) for k in range(down)]
+
+    @pl.when(inner == 0)
+    def _():
+        msg_j[...] = joined(leads[0][HD + 1 : HD + 2], leads[0], leads[1:])
+
+    @pl.when(inner == 1)
+    def _():
+        msg_j[...] = joined(id0, own_l, leads[:1])
+
+    j_copy.start()
+
     loads[6].wait()
     q_parts = [None, None]
     for t in range(FC):
         rows = slice(t * TF, (t + 1) * TF)
         q_parts.append(rotated(q_ref[rows, :], time_own[t : t + 1, :], time_own[8 + t : 9 + t, :]))
-
-    base[...] = jnp.zeros_like(own_t)
-    for i in range(steps):
-
-        @pl.when(outer // 2**i % 2 == 1)
-        def _(i=i):
-            t_copies[i, 1].wait_recv()
-            base[...] += recv_t[i].astype(F32)
-
-        if i + 1 < steps:
-            msg_t[i + 1] = (base[...] + own_t).astype(BF16)
-            t_start(i + 1)
-
-    earlier = base[...]
-    msg_r[...] = (earlier + jnp.where(inner == 0, 1.0, 0.0) * own_t).astype(BF16)
-    r_copy.start()
-
-    for k in range(1, down + 1):
-
-        @pl.when(l_gets[k])
-        def _(k=k):
-            l_copies[k].wait_recv()
-
-        @pl.when(jnp.logical_not(l_gets[k]))
-        def _(k=k):
-            recv_l[k - 1] = tagged(jnp.zeros_like(own_t), -1.0, -1.0)
-
-    def joined(ident, total, pieces):
-        for piece in pieces:
-            total = total + jnp.where(piece[HD + 1 : HD + 2] == ident, 1.0, 0.0) * piece
-        return tagged(total, ident, ident)
-
-    leads = [recv_l[k].astype(F32) for k in range(down)]
-
-    @pl.when(inner == 0)
-    def _():
-        msg_j[...] = joined(leads[0][HD + 1 : HD + 2], leads[0], leads[1:])
-
-    @pl.when(inner == 1)
-    def _():
-        msg_j[...] = joined(id0, own_l, leads[:1])
-
-    j_copy.start()
 
     @pl.when(f > 0)
     def _():

time: 42.3 us -> 42.3 us (level)
  no operation moved by 1% of the time
where the time goes in v3:
time: 42.3 us; the launch traced here: 42.2 us
  Pallas kernels  40.3 us (95%)
  local copies, waits for them, and re-layouts  1.92 us (5%)
    pallas_call x1, Pallas kernels, per_device(): pl.pallas_call(functools.partial(kernel, (F, Y, heads, HG, W, tuple(chunk...  40.3 us
    unnamed x1, local copies, waits for them, and re-layouts  1.92 us

profile of v3, /device:TPU:17, one launch (start us, length us, event | category | flops | bytes accessed | tf_op | source)
XLA Modules:
  0.0 42.2 jit_solution(8398397465567099081)
XLA Ops:
  0.0 40.3 %attend_conv.1 = bf16[2,2,32,2240]{3,2,1,0:T(8,128)(2,1)} custom-call(bf16[512,224]{1,0:T(8,128)(2,1)} %bitcast.3, bf16[512,224]{1,0:T(8,128)(2,1)} %bitcast.4, bf16[512,224]{1,0:T(8,128)(2,1)} %bitcast.5, s32[2]{0:T(128)} %fi_any.1, s32[8]{0:T(128)} %hi_any.1, s32[32]{0:T(128)} %wi_any.1, s32[2]{0:T(128)} %fb_any.1, bf16[3,224,2240]{2,1,0:T(8,128)(2,1)} %w_ref.1, ...), custom_call_target="tpu_custom_call" | custom-call | tf_op jit(solution)/shard_map/attend_conv/pallas_call | solution.py:430
  40.3 1.9 %copy.11 = bf16[2,2,32,2240]{3,2,1,0:T(8,128)(2,1)} copy(bf16[2,2,32,2240]{3,2,1,0:T(8,128)(2,1)} %attend_conv.1) | data formatting | bytes 1146880

commit v4 on v1

--- a/solution.py
+++ b/solution.py
@@ -128,6 +128,17 @@
     w_local = pltpu.make_async_copy(w_ref, w_buf.at[0], w_sem)
     w_local.start()
 
+    pl.semaphore_wait(barrier, (F - 1) + 1 + (Y - 1))
+
+    w_far = remote(w_ref, w_buf.at[1], w_send, w_recv, f, mate)
+    nxt = lax.rem(f + 1, F)
+    q_copy = remote(q_any, qh, halo_send.at[0], halo_recv.at[0], nxt, h)
+    t_copy = remote(time_own, time_prev, halo_send.at[1], halo_recv.at[1], nxt, h)
+
+    @pl.when(f < F - 1)
+    def _():
+        q_copy.start()
+
     lanes = heads * PAD
     spread, swap, gather, freqs, masks = tables(heads)
     for load in loads[:4]:
@@ -142,16 +153,8 @@
     ).reshape(TF, lanes)
     sin_hw = (jnp.sin(h_ang).reshape(HG, 1, lanes) + jnp.sin(w_ang).reshape(1, W, lanes)).reshape(TF, lanes)
 
-    pl.semaphore_wait(barrier, (F - 1) + 1 + (Y - 1))
-
-    w_far = remote(w_ref, w_buf.at[1], w_send, w_recv, f, mate)
-    nxt = lax.rem(f + 1, F)
-    q_copy = remote(q_any, qh, halo_send.at[0], halo_recv.at[0], nxt, h)
-    t_copy = remote(time_own, time_prev, halo_send.at[1], halo_recv.at[1], nxt, h)
-
     @pl.when(f < F - 1)
     def _():
-        q_copy.start()
         t_copy.start()
 
     @pl.when(f == 0)
@@ -230,56 +233,56 @@
 
     w_far.start()
 
+    @pl.when(inner == 0)
+    def _():
+        base[...] = own_t
+
+    @pl.when(inner == 1)
+    def _():
+        base[...] = jnp.zeros_like(own_t)
+
+    for k in range(1, O):
+
+        @pl.when(outer >= k)
+        def _(k=k):
+            t_copies[k].wait_recv()
+            base[...] += recv_t[k - 1].astype(F32)
+
+    msg_r[...] = base[...].astype(BF16)
+    r_copy.start()
+
+    for k in range(1, down + 1):
+
+        @pl.when(l_gets[k])
+        def _(k=k):
+            l_copies[k].wait_recv()
+
+        @pl.when(jnp.logical_not(l_gets[k]))
+        def _(k=k):
+            recv_l[k - 1] = tagged(jnp.zeros_like(own_t), -1.0, -1.0)
+
+    def joined(ident, total, pieces):
+        for piece in pieces:
+            total = total + jnp.where(piece[HD + 1 : HD + 2] == ident, 1.0, 0.0) * piece
+        return tagged(total, ident, ident)
+
+    leads = [recv_l[k].astype(F32) for k in range(down)]
+
+    @pl.when(inner == 0)
+    def _():
+        msg_j[...] = joined(leads[0][HD + 1 : HD + 2], leads[0], leads[1:])
+
+    @pl.when(inner == 1)
+    def _():
+        msg_j[...] = joined(id0, own_l, leads[:1])
+
+    j_copy.start()
+
     loads[6].wait()
     q_parts = [None, None]
     for t in range(FC):
         rows = slice(t * TF, (t + 1) * TF)
         q_parts.append(rotated(q_ref[rows, :], time_own[t : t + 1, :], time_own[8 + t : 9 + t, :]))
-
-    @pl.when(inner == 0)
-    def _():
-        base[...] = own_t
-
-    @pl.when(inner == 1)
-    def _():
-        base[...] = jnp.zeros_like(own_t)
-
-    for k in range(1, O):
-
-        @pl.when(outer >= k)
-        def _(k=k):
-            t_copies[k].wait_recv()
-            base[...] += recv_t[k - 1].astype(F32)
-
-    msg_r[...] = base[...].astype(BF16)
-    r_copy.start()
-
-    for k in range(1, down + 1):
-
-        @pl.when(l_gets[k])
-        def _(k=k):
-            l_copies[k].wait_recv()
-
-        @pl.when(jnp.logical_not(l_gets[k]))
-        def _(k=k):
-            recv_l[k - 1] = tagged(jnp.zeros_like(own_t), -1.0, -1.0)
-
-    def joined(ident, total, pieces):
-        for piece in pieces:
-            total = total + jnp.where(piece[HD + 1 : HD + 2] == ident, 1.0, 0.0) * piece
-        return tagged(total, ident, ident)
-
-    leads = [recv_l[k].astype(F32) for k in range(down)]
-
-    @pl.when(inner == 0)
-    def _():
-        msg_j[...] = joined(leads[0][HD + 1 : HD + 2], leads[0], leads[1:])
-
-    @pl.when(inner == 1)
-    def _():
-        msg_j[...] = joined(id0, own_l, leads[:1])
-
-    j_copy.start()
 
     @pl.when(f > 0)
     def _():

time: 42.1 us -> 42.2 us (level)
  no operation moved by 1% of the time
where the time goes in v4:
time: 42.2 us; the launch traced here: 42 us
  Pallas kernels  40.1 us (95%)
  local copies, waits for them, and re-layouts  1.92 us (5%)
    pallas_call x1, Pallas kernels, per_device(): pl.pallas_call(functools.partial(kernel, (F, Y, heads, HG, W, tuple(chunk...  40.1 us
    unnamed x1, local copies, waits for them, and re-layouts  1.92 us

profile of v4, /device:TPU:17, one launch (start us, length us, event | category | flops | bytes accessed | tf_op | source)
XLA Modules:
  0.0 42.0 jit_solution(8332110149374684105)
XLA Ops:
  0.0 40.1 %attend_conv.1 = bf16[2,2,32,2240]{3,2,1,0:T(8,128)(2,1)} custom-call(bf16[512,224]{1,0:T(8,128)(2,1)} %bitcast.3, bf16[512,224]{1,0:T(8,128)(2,1)} %bitcast.4, bf16[512,224]{1,0:T(8,128)(2,1)} %bitcast.5, s32[2]{0:T(128)} %fi_any.1, s32[8]{0:T(128)} %hi_any.1, s32[32]{0:T(128)} %wi_any.1, s32[2]{0:T(128)} %fb_any.1, bf16[3,224,2240]{2,1,0:T(8,128)(2,1)} %w_ref.1, ...), custom_call_target="tpu_custom_call" | custom-call | tf_op jit(solution)/shard_map/attend_conv/pallas_call | solution.py:423
  40.1 1.9 %copy.11 = bf16[2,2,32,2240]{3,2,1,0:T(8,128)(2,1)} copy(bf16[2,2,32,2240]{3,2,1,0:T(8,128)(2,1)} %attend_conv.1) | data formatting | bytes 1146880
